TPU v7x, 32 devices: a whole 2x2x4 slice. The times are simulated.
32 devices in a mesh: dp: 4 (over x, core), seq: 8 (over z, y).
Axes of the slice: x: 2, y: 2, z: 4, core: 2. Of those that a mesh axis runs over, the one named last changes fastest.
Arguments:
- inputs: bfloat16 [4, 4096, 768], P('dp', 'seq'), may hold values from -6 to 6
- block_mix: bfloat16 [8, 512, 512], P('seq'), may hold values from -0.25 to 0.25
- cross_mix: bfloat16 [512, 8, 8], P('seq'), may hold values from -2 to 2
- cotangent: bfloat16 [4, 4096, 768], P('dp', 'seq'), may hold values from -0.59765625 to 0.59765625
Outputs:
- output: bfloat16 [4, 4096, 768], P('dp', 'seq')
- input_grad: bfloat16 [4, 4096, 768], P('dp', 'seq')
- block_grad: bfloat16 [8, 512, 512], P('seq')
- cross_grad: bfloat16 [512, 8, 8], P('seq')
All inputs are finite; a program needn't handle non-finite values.
Results may differ from a plain program's by a relative error of at most 0.012.
Values may be sent and summed in bfloat16 or wider, within the bound.
A program may use at most 64 MiB of HBM per device.

v0:
```python
import jax
import jax.numpy as jnp
from jax import lax
from jax.sharding import PartitionSpec as P


def local(inputs, block_mix, cross_mix, cotangent):
    h = jnp.einsum("bsr,brc->bsc", block_mix, inputs, preferred_element_type=jnp.float32).astype(
        jnp.bfloat16
    )
    gate = jax.nn.sigmoid(inputs.astype(jnp.float32))
    h_cols = lax.all_to_all(h, "seq", split_axis=1, concat_axis=0, tiled=True)
    z_cols = jnp.einsum(
        "rab,brc->arc", cross_mix, h_cols, preferred_element_type=jnp.float32
    ).astype(jnp.bfloat16)
    z = lax.all_to_all(z_cols, "seq", split_axis=0, concat_axis=1, tiled=True)
    dz = (cotangent.astype(jnp.float32) * gate).astype(jnp.bfloat16)
    dz_cols = lax.all_to_all(dz, "seq", split_axis=1, concat_axis=0, tiled=True)
    dh_cols = jnp.einsum(
        "rab,arc->brc", cross_mix, dz_cols, preferred_element_type=jnp.float32
    ).astype(jnp.bfloat16)
    cross_part = jnp.einsum("arc,brc->rab", dz_cols, h_cols, preferred_element_type=jnp.float32)
    dh = lax.all_to_all(dh_cols, "seq", split_axis=0, concat_axis=1, tiled=True)
    dv = jnp.einsum("bsr,bsc->brc", block_mix, dh, preferred_element_type=jnp.float32)
    block_part = jnp.einsum("bsc,brc->bsr", dh, inputs, preferred_element_type=jnp.float32)
    block_sum, cross_sum = (
        lax.psum(block_part.astype(jnp.bfloat16), "dp").astype(jnp.float32),
        lax.psum(cross_part.astype(jnp.bfloat16), "dp").astype(jnp.float32),
    )
    zf = z.astype(jnp.float32)
    output = (inputs.astype(jnp.float32) + zf * gate).astype(jnp.bfloat16)
    input_grad = (cotangent.astype(jnp.float32) * (1.0 + zf * gate * (1.0 - gate)) + dv).astype(
        jnp.bfloat16
    )
    return (output, input_grad, block_sum.astype(jnp.bfloat16), cross_sum.astype(jnp.bfloat16))


def solution(mesh):
    placed = (
        P("dp", "seq", None),
        P("seq", None, None),
        P("seq", None, None),
        P("dp", "seq", None),
    )
    return jax.shard_map(
        local,
        mesh=mesh,
        in_specs=placed,
        out_specs=(
            P("dp", "seq", None),
            P("dp", "seq", None),
            P("seq", None, None),
            P("seq", None, None),
        ),
        check_vma=False,
    )
```

profile of v0, /device:TPU:0, one launch (start us, length us, event | category | flops | bytes accessed | tf_op | source)
XLA Modules:
  0.0 190.0 jit_solution(17759699037681168629)
XLA Ops:
  7.2 0.0 copy-start
  7.2 1.0 copy-done
  8.2 1.7 fusion.9
  9.9 1.2 copy.73
  11.1 0.5 broadcast.12
  11.7 5.4 %reduce = bf16[512,768]{1,0:T(8,128)(2,1)S(1)} reduce(bf16[512,1,768]{2,1,0:T(2,128)(2,1)S(1)} %bitcast.39, bf16[]{:T(256)} %broadcast.12), dimensions={1}, to_apply=%bitcast.37.reduce_sub_computation | reduce | bytes 1572866
  17.1 0.0 copy-start.8
  17.1 1.1 reshape.57
  18.2 7.3 %all-to-all-start = ((bf16[8,2,24576]{2,1,0:T(2,128)(2,1)}), bf16[8,2,24576]{2,1,0:T(2,128)(2,1)S(1)}, u32[]{:S(2)}, u32[]{:S(2)}) async-start(bf16[8,2,24576]{2,1,0:T(2,128)(2,1)} %reshape.57), calls=%async_computation | async-start | bytes 1572864 | tf_op jit(solution)/shard_map/all_to_all | solution.py:12
  25.4 0.1 copy.55
  25.6 20.0 %all-to-all-done = bf16[8,2,24576]{2,1,0:T(2,128)(2,1)S(1)} async-done(((bf16[8,2,24576]{2,1,0:T(2,128)(2,1)}), bf16[8,2,24576]{2,1,0:T(2,128)(2,1)S(1)}, u32[]{:S(2)}, u32[]{:S(2)}) %all-to-all-start) | async-done | bytes 786464 | tf_op jit(solution)/shard_map/all_to_all | solution.py:12
  45.6 0.8 reshape.58
  46.4 0.1 copy.62
  46.6 0.0 copy-start.4
  46.6 0.9 copy-done.4
  47.4 0.6 fusion.7
  48.0 1.0 copy.50
  49.1 3.9 %all-to-all-start.1 = ((bf16[8,64,768]{2,1,0:T(8,128)(2,1)}), bf16[8,64,768]{2,1,0:T(8,128)(2,1)S(1)}, u32[]{:S(2)}, u32[]{:S(2)}) async-start(bf16[8,64,768]{2,1,0:T(8,128)(2,1)} %copy.50), calls=%async_computation.1 | async-start | bytes 1572864 | tf_op jit(solution)/shard_map/all_to_all | solution.py:16
  52.9 1.4 copy.46
  54.3 0.0 copy-done.7
  54.4 1.2 copy.52
  55.5 17.6 %all-to-all-done.1 = bf16[8,64,768]{2,1,0:T(8,128)(2,1)S(1)} async-done(((bf16[8,64,768]{2,1,0:T(8,128)(2,1)}), bf16[8,64,768]{2,1,0:T(8,128)(2,1)S(1)}, u32[]{:S(2)}, u32[]{:S(2)}) %all-to-all-start.1) | async-done | bytes 786464 | tf_op jit(solution)/shard_map/all_to_all | solution.py:16
  73.1 0.9 copy-done.3
  74.0 1.2 bitcast_convert_fusion
  75.2 1.6 copy.51
  76.8 3.4 %fusion.6 = (bf16[1,512,768]{1,2,0:T(8,128)(2,1)}, bf16[1,512,768]{1,2,0:T(8,128)(2,1)}) fusion(bf16[1,512,768]{1,2,0:T(8,128)(2,1)} %copy.52, bf16[1,512,768]{1,2,0:T(8,128)(2,1)S(1)} %copy.46, f32[1,512,768]{1,2,0:T(8,128)} %copy.51), kind=kLoop, calls=%fused_computation.10 | loop fusion | flops 3932160 | bytes 4718592 | tf_op jit(solution)/shard_map/convert_element_type | solution.py:17
  80.2 3.7 %copy.53 = bf16[1,512,768]{2,0,1:T(2,128)(2,1)S(1)} copy(bf16[1,512,768]{1,2,0:T(8,128)(2,1)} %get-tuple-element.20) | data formatting | bytes 1572864 | tf_op jit(solution)/shard_map/convert_element_type | solution.py:17
  84.0 6.3 %reduce.1 = bf16[512,768]{1,0:T(8,128)(2,1)} reduce(bf16[512,1,768]{2,1,0:T(2,128)(2,1)S(1)} %bitcast.40, bf16[]{:T(256)} %broadcast.12), dimensions={1}, to_apply=%bitcast.30.reduce_sub_computation | reduce | bytes 1572866
  90.3 2.2 %reshape.59 = bf16[8,2,24576]{2,1,0:T(2,128)(2,1)S(1)} reshape(bf16[512,768]{1,0:T(8,128)(2,1)} %reduce.1) | data formatting | bytes 1572864
  92.5 23.8 %all_to_all.42 = bf16[8,2,24576]{2,1,0:T(2,128)(2,1)} all-to-all(bf16[8,2,24576]{2,1,0:T(2,128)(2,1)S(1)} %reshape.59), channel_id=1, replica_groups=mesh['dp'=4,'seq'=8] {'seq'}, dimensions={0} | all-to-all | bytes 1572864 | tf_op jit(solution)/shard_map/all_to_all | solution.py:18
  116.3 4.1 %reshape.60 = bf16[512,1,768]{2,1,0:T(2,128)(2,1)S(1)} reshape(bf16[8,2,24576]{2,1,0:T(2,128)(2,1)} %all_to_all.42) | data formatting | bytes 1572864
  120.4 0.1 copy.63
  120.5 0.6 fusion.8
  121.1 0.3 copy-done.6
  121.4 1.0 copy.56
  122.5 4.3 %all-to-all-start.3 = ((bf16[8,64,768]{2,1,0:T(8,128)(2,1)}), bf16[8,64,768]{2,1,0:T(8,128)(2,1)}, u32[]{:S(2)}, u32[]{:S(2)}) async-start(bf16[8,64,768]{2,1,0:T(8,128)(2,1)} %copy.56), calls=%async_computation.3 | async-start | bytes 1572864 | tf_op jit(solution)/shard_map/all_to_all | solution.py:23
  126.8 0.0 all-reduce.2.cloned.1.call-start
  126.9 1.2 copy.59
  128.0 2.1 %convolution_convert_fusion.4 = bf16[64,8,8]{2,1,0:T(8,128)(2,1)S(1)} fusion(bf16[8,64,768]{2,1,0:T(8,128)(2,1)} %bitcast.47, bf16[8,64,768]{2,1,0:T(8,128)(2,1)S(1)} %bitcast.45), kind=kOutput, calls=%fused_computation.19 | convolution fusion | flops 6295552 | bytes 1581056 | tf_op jit(solution)/shard_map/arc,brc->rab/dot_general | solution.py:22
  130.1 12.4 %psum.15 = bf16[64,8,8]{2,1,0:T(8,128)(2,1)S(1)} all-reduce(bf16[64,8,8]{2,1,0:T(8,128)(2,1)S(1)} %convolution_convert_fusion.4), channel_id=1, replica_groups=mesh['dp'=4,'seq'=8] {'dp'}, use_global_device_ids=true, to_apply=%region_1.0 | all-reduce | flops 4096 | bytes 16384 | tf_op jit(solution)/shard_map/psum | solution.py:28
  142.5 0.7 copy.61
  143.2 3.0 %all-to-all-done.3 = bf16[8,64,768]{2,1,0:T(8,128)(2,1)} async-done(((bf16[8,64,768]{2,1,0:T(8,128)(2,1)}), bf16[8,64,768]{2,1,0:T(8,128)(2,1)}, u32[]{:S(2)}, u32[]{:S(2)}) %all-to-all-start.3) | async-done | bytes 786464 | tf_op jit(solution)/shard_map/all_to_all | solution.py:23
  146.2 2.8 %fusion.10 = bf16[1,512,512]{2,1,0:T(8,128)(2,1)} fusion(bf16[512,768]{1,0:T(8,128)(2,1)} %bitcast.6, bf16[1,512,768]{2,1,0:T(8,128)(2,1)} %param.4), kind=kOutput, calls=%fused_computation.18 | convolution fusion | flops 402915328 | bytes 2097152 | tf_op jit(solution)/shard_map/bsc,brc->bsr/dot_general | solution.py:25
  149.0 0.0 all-reduce.2.cloned.1.call-update
  149.0 3.2 %fusion.5 = bf16[1,512,768]{1,2,0:T(8,128)(2,1)} fusion(bf16[1,512,768]{1,2,0:T(8,128)(2,1)} %copy.52, bf16[512,768]{1,0:T(8,128)(2,1)} %bitcast.6, f32[1,512,768]{1,2,0:T(8,128)S(1)} %copy-done.1, bf16[1,512,512]{2,1,0:T(8,128)(2,1)S(1)} %copy-done, bf16[1,512,768]{1,2,0:T(8,128)(2,1)S(1)} %copy.46), kind=kOutput, calls=%fused_computation.9 | convolution fusion | flops 407371776 | bytes 5242880 | tf_op jit(solution)/shard_map/bsr,bsc->brc/dot_general | solution.py:24
  152.3 2.3 %copy.60 = bf16[1,512,768]{2,1,0:T(8,128)(2,1)} copy(bf16[1,512,768]{1,2,0:T(8,128)(2,1)} %fusion.5) | data formatting | bytes 1572864
  154.6 26.8 %all-reduce.2.cloned.1.call-done = bf16[1,512,512]{2,1,0:T(8,128)(2,1)} async-done(((bf16[1,512,512]{2,1,0:T(8,128)(2,1)}), bf16[1,512,512]{2,1,0:T(8,128)(2,1)}) %all-reduce.2.cloned.1.call-update) | async-done | bytes 524304 | tf_op jit(solution)/shard_map/psum | solution.py:27
  181.3 1.9 copy.75
  (10 shorter events, 0.0 us)
Async XLA Ops:
  7.2 1.0 copy-start
  17.1 8.4 %copy-start.8 = (bf16[64,8,8]{0,2,1:T(8,128)(2,1)S(1)}, bf16[64,8,8]{0,2,1:T(8,128)(2,1)}, u32[]{:S(2)}) copy-start(bf16[64,8,8]{0,2,1:T(8,128)(2,1)} %param.6) | copy-start | bytes 24580
  18.2 27.5 %all-to-all-start = ((bf16[8,2,24576]{2,1,0:T(2,128)(2,1)}), bf16[8,2,24576]{2,1,0:T(2,128)(2,1)S(1)}, u32[]{:S(2)}, u32[]{:S(2)}) async-start(bf16[8,2,24576]{2,1,0:T(2,128)(2,1)} %reshape.57), calls=%async_computation | async-start | bytes 1572864 | tf_op jit(solution)/shard_map/all_to_all | solution.py:12
  46.6 0.9 copy-start.4
  49.1 5.3 %copy-start.7 = (bf16[1,512,768]{2,1,0:T(8,128)(2,1)S(1)}, bf16[1,512,768]{2,1,0:T(8,128)(2,1)}, u32[]{:S(2)}) copy-start(bf16[1,512,768]{2,1,0:T(8,128)(2,1)} %param.7) | copy-start | bytes 2359300
  49.1 24.0 %all-to-all-start.1 = ((bf16[8,64,768]{2,1,0:T(8,128)(2,1)}), bf16[8,64,768]{2,1,0:T(8,128)(2,1)S(1)}, u32[]{:S(2)}, u32[]{:S(2)}) async-start(bf16[8,64,768]{2,1,0:T(8,128)(2,1)} %copy.50), calls=%async_computation.1 | async-start | bytes 1572864 | tf_op jit(solution)/shard_map/all_to_all | solution.py:16
  73.1 0.9 copy-start.3
  120.5 0.9 copy-start.6
  121.4 5.4 %copy-start.2 = (bf16[1,512,768]{1,2,0:T(8,128)(2,1)S(1)}, bf16[1,512,768]{1,2,0:T(8,128)(2,1)}, u32[]{:S(2)}) copy-start(bf16[1,512,768]{1,2,0:T(8,128)(2,1)} %get-tuple-element.21) | copy-start | bytes 2359300
  122.5 5.6 %copy-start.5 = (bf16[1,512,768]{2,1,0:T(8,128)(2,1)S(1)}, bf16[1,512,768]{2,1,0:T(8,128)(2,1)}, u32[]{:S(2)}) copy-start(bf16[1,512,768]{2,1,0:T(8,128)(2,1)} %copy-done.4) | copy-start | bytes 2359300
  122.5 23.8 %all-to-all-start.3 = ((bf16[8,64,768]{2,1,0:T(8,128)(2,1)}), bf16[8,64,768]{2,1,0:T(8,128)(2,1)}, u32[]{:S(2)}, u32[]{:S(2)}) async-start(bf16[8,64,768]{2,1,0:T(8,128)(2,1)} %copy.56), calls=%async_computation.3 | async-start | bytes 1572864 | tf_op jit(solution)/shard_map/all_to_all | solution.py:23
  126.8 54.5 %all-reduce.2.cloned.1.call-start = ((), (), s32[]{:S(2)}) async-start(), calls=%async_computation.4 | async-start | bytes 1048576 | tf_op jit(solution)/shard_map/psum | solution.py:27
  142.5 6.5 %copy-start.1 = (f32[1,512,768]{1,2,0:T(8,128)S(1)}, f32[1,512,768]{1,2,0:T(8,128)}, u32[]{:S(2)}) copy-start(f32[1,512,768]{1,2,0:T(8,128)} %copy.51) | copy-start | bytes 4718596
Sparse Core Ops, SparseCore 0:
  149.2 32.1 all-reduce.1
where the time goes:
time: 191 us; the launch traced here: 190 us
  waiting for transfers between devices  67.4 us (35%)
  blocking collectives  36.1 us (19%)
  local copies, waits for them, and re-layouts  29.5 us (15%)
  other arithmetic  16.4 us (9%)
  starting transfers between devices  15.5 us (8%)
  between operations  14.2 us (7%)
  matrix products  10.9 us (6%)
    psum x1, waiting for transfers between devices, local(): lax.psum(block_part.astype(jnp.bfloat16), 'dp').astype(jnp.float32)  26.8 us
    all_to_all x1, blocking collectives, local(): dz_cols = lax.all_to_all(dz, 'seq', split_axis=1, concat_axis=0, tiled=True)  23.8 us
    unnamed x32, local copies, waits for them, and re-layouts  20.9 us
    all_to_all x1, waiting for transfers between devices, local(): h_cols = lax.all_to_all(h, 'seq', split_axis=1, concat_axis=0, tiled=True)  20 us
    all_to_all x1, waiting for transfers between devices, local(): z = lax.all_to_all(z_cols, 'seq', split_axis=0, concat_axis=1, tiled=True)  17.6 us
    psum x1, blocking collectives, local(): lax.psum(cross_part.astype(jnp.bfloat16), 'dp').astype(jnp.float32)  12.4 us
    unnamed x2, other arithmetic  11.7 us
    all_to_all x1, starting transfers between devices, local(): h_cols = lax.all_to_all(h, 'seq', split_axis=1, concat_axis=0, tiled=True)  7.28 us
  transfers between devices with their start and end apart: 4, of which 4 were waited for; matrix products, arithmetic and copies ran while one was open for 6% of the time, Pallas kernels for 0%

commit v1 on v0

--- a/solution.py
+++ b/solution.py
@@ -13,7 +13,15 @@
     z_cols = jnp.einsum(
         "rab,brc->arc", cross_mix, h_cols, preferred_element_type=jnp.float32
     ).astype(jnp.bfloat16)
-    z = lax.all_to_all(z_cols, "seq", split_axis=0, concat_axis=1, tiled=True)
+    ways, here = (lax.axis_size("seq"), lax.axis_index("seq"))
+    width = z_cols.shape[0] // ways
+    turned = jnp.roll(z_cols, -here * width, axis=0)
+    got = [lax.slice_in_dim(turned, 0, width, axis=0)]
+    for far in range(1, ways):
+        sent = lax.slice_in_dim(turned, far * width, (far + 1) * width, axis=0)
+        got.append(lax.ppermute(sent, "seq", [(d, (d + far) % ways) for d in range(ways)]))
+    line = jnp.concatenate(got[::-1], axis=1)
+    z = jnp.roll(line, (here + 1) * got[0].shape[1], axis=1)
     dz = (cotangent.astype(jnp.float32) * gate).astype(jnp.bfloat16)
     dz_cols = lax.all_to_all(dz, "seq", split_axis=1, concat_axis=0, tiled=True)
     dh_cols = jnp.einsum(

time: 191 us -> 178 us (0.932)
  local copies, waits for them, and re-layouts: 29.5 us -> 12.7 us
  starting transfers between devices: 15.5 us -> 29.3 us
  waiting for transfers between devices: 67.4 us -> 62.7 us
  other arithmetic: 16.4 us -> 12.7 us
    ppermute x0 -> x7, starting transfers between devices: none -> 18.4 us  [local(): lax.ppermute(sent, 'seq', [(d, (d + far) % ways) for d in range(ways)])]
    all_to_all x1 -> x0, waiting for transfers between devices: 17.6 us -> none  [local(): z = lax.all_to_all(z_cols, 'seq', split_axis=0, concat_axis=1, tiled=True)]
    unnamed x32 -> x43, local copies, waits for them, and re-layouts: 20.9 us -> 8.4 us
    ppermute x0 -> x7, waiting for transfers between devices: none -> 7.42 us  [local(): lax.ppermute(sent, 'seq', [(d, (d + far) % ways) for d in range(ways)])]
    all_to_all x1 -> x0, starting transfers between devices: 3.86 us -> none  [local(): z = lax.all_to_all(z_cols, 'seq', split_axis=0, concat_axis=1, tiled=True)]
    all_to_all x1, waiting for transfers between devices: 3.01 us -> 6.09 us  [local(): dh = lax.all_to_all(dh_cols, 'seq', split_axis=0, concat_axis=1, tiled=True)]
    convert_element_type x2 -> x0, local copies, waits for them, and re-layouts: 2.63 us -> none  [the longest x1 1.62 us: local(): zf = z.astype(jnp.float32)]
    convert_element_type x1, local copies, waits for them, and re-layouts: 3.72 us -> 1.21 us  [local(): dz = (cotangent.astype(jnp.float32) * gate).astype(jnp.bfloat16)]
  transfers between devices with their start and end apart: 4 -> 10, of which waited for: 4 -> 5; matrix products, arithmetic and copies ran while one was open for 6% -> 3% of each run, Pallas kernels for 0% -> 0%
where the time goes in v1:
time: 178 us; the launch traced here: 177 us
  waiting for transfers between devices  62.7 us (35%)
  blocking collectives  36 us (20%)
  starting transfers between devices  29.3 us (16%)
  between operations  14.4 us (8%)
  local copies, waits for them, and re-layouts  12.7 us (7%)
  other arithmetic  12.7 us (7%)
  matrix products  9.37 us (5%)
    psum x1, waiting for transfers between devices, local(): lax.psum(block_part.astype(jnp.bfloat16), 'dp').astype(jnp.float32)  29.2 us
    all_to_all x1, blocking collectives, local(): dz_cols = lax.all_to_all(dz, 'seq', split_axis=1, concat_axis=0, tiled=True)  24.1 us
    all_to_all x1, waiting for transfers between devices, local(): h_cols = lax.all_to_all(h, 'seq', split_axis=1, concat_axis=0, tiled=True)  20 us
    ppermute x7, starting transfers between devices, local(): lax.ppermute(sent, 'seq', [(d, (d + far) % ways) for d in range(ways)])  18.4 us
    psum x1, blocking collectives, local(): lax.psum(cross_part.astype(jnp.bfloat16), 'dp').astype(jnp.float32)  11.9 us
    unnamed x2, other arithmetic  10.9 us
    unnamed x43, local copies, waits for them, and re-layouts  8.4 us
    ppermute x7, waiting for transfers between devices, local(): lax.ppermute(sent, 'seq', [(d, (d + far) % ways) for d in range(ways)])  7.42 us
  transfers between devices with their start and end apart: 10, of which 5 were waited for; matrix products, arithmetic and copies ran while one was open for 3% of the time, Pallas kernels for 0%

profile of v1, /device:TPU:0, one launch (start us, length us, event | category | flops | bytes accessed | tf_op | source)
XLA Modules:
  0.0 177.2 jit_solution(1749609339046484815)
XLA Ops:
  7.2 0.0 copy-start
  7.2 1.0 copy-done
  8.2 1.7 fusion.8
  9.9 1.2 copy.100
  11.1 0.5 broadcast.14
  11.7 5.4 %reduce = bf16[512,768]{1,0:T(8,128)(2,1)S(1)} reduce(bf16[512,1,768]{2,1,0:T(2,128)(2,1)S(1)} %bitcast.38, bf16[]{:T(256)} %broadcast.14), dimensions={1}, to_apply=%bitcast.37.reduce_sub_computation | reduce | bytes 1572866
  17.1 0.0 copy-start.8
  17.1 1.1 reshape.39
  18.2 7.3 %all-to-all-start = ((bf16[8,2,24576]{2,1,0:T(2,128)(2,1)}), bf16[8,2,24576]{2,1,0:T(2,128)(2,1)S(1)}, u32[]{:S(2)}, u32[]{:S(2)}) async-start(bf16[8,2,24576]{2,1,0:T(2,128)(2,1)} %reshape.39), calls=%async_computation | async-start | bytes 1572864 | tf_op jit(solution)/shard_map/all_to_all | solution.py:12
  25.4 0.1 copy.76
  25.6 20.0 %all-to-all-done = bf16[8,2,24576]{2,1,0:T(2,128)(2,1)S(1)} async-done(((bf16[8,2,24576]{2,1,0:T(2,128)(2,1)}), bf16[8,2,24576]{2,1,0:T(2,128)(2,1)S(1)}, u32[]{:S(2)}, u32[]{:S(2)}) %all-to-all-start) | async-done | bytes 786464 | tf_op jit(solution)/shard_map/all_to_all | solution.py:12
  45.6 0.8 reshape.40
  46.4 0.1 copy.83
  46.6 0.9 copy-done.1
  47.4 0.6 fusion.17
  48.0 0.1 copy.98
  48.2 0.3 fusion.11
  48.5 0.7 fusion.21
  49.2 2.3 %collective-permute-start = (bf16[1,64,768]{2,1,0:T(8,128)(2,1)S(1)}, bf16[1,64,768]{2,1,0:T(8,128)(2,1)S(1)}, u32[]{:S(2)}, u32[]{:S(2)}) collective-permute-start(bf16[1,64,768]{2,1,0:T(8,128)(2,1)S(1)} %get-tuple-element.36), channel_id=1, source_target_pairs={{0,7},{1,0},{2,1},{3,2},{4,3},{5,4},{6,5},{7,6},{8,15},{9,8},{10,9... | collective-permute-start | bytes 294920 | tf_op jit(solution)/shard_map/ppermute | solution.py:22
  51.5 0.6 collective-permute-start.5
  52.1 1.1 collective-permute-start.4
  53.2 4.2 %collective-permute-start.3 = (bf16[1,64,768]{2,1,0:T(8,128)(2,1)S(1)}, bf16[1,64,768]{2,1,0:T(8,128)(2,1)S(1)}, u32[]{:S(2)}, u32[]{:S(2)}) collective-permute-start(bf16[1,64,768]{2,1,0:T(8,128)(2,1)S(1)} %get-tuple-element.33), channel_id=1, source_target_pairs={{0,4},{1,5},{2,6},{3,7},{4,0},{5,1},{6,2},{7,3},{8,12},{9,13},{10,... | collective-permute-start | bytes 294920 | tf_op jit(solution)/shard_map/ppermute | solution.py:22
  57.3 2.4 %collective-permute-start.1 = (bf16[1,64,768]{2,1,0:T(8,128)(2,1)}, bf16[1,64,768]{2,1,0:T(8,128)(2,1)S(1)}, u32[]{:S(2)}, u32[]{:S(2)}) collective-permute-start(bf16[1,64,768]{2,1,0:T(8,128)(2,1)} %get-tuple-element.35), channel_id=1, source_target_pairs={{0,6},{1,7},{2,0},{3,1},{4,2},{5,3},{6,4},{7,5},{8,14},{9,15},{10,... | collective-permute-start | bytes 294920 | tf_op jit(solution)/shard_map/ppermute | solution.py:22
  59.7 3.3 %collective-permute-done.1 = bf16[1,64,768]{2,1,0:T(8,128)(2,1)S(1)} collective-permute-done((bf16[1,64,768]{2,1,0:T(8,128)(2,1)}, bf16[1,64,768]{2,1,0:T(8,128)(2,1)S(1)}, u32[]{:S(2)}, u32[]{:S(2)}) %collective-permute-start.1) | collective-permute-done | bytes 98336 | tf_op jit(solution)/shard_map/ppermute | solution.py:22
  63.0 7.9 %collective-permute-start.2 = (bf16[1,64,768]{2,1,0:T(8,128)(2,1)}, bf16[1,64,768]{2,1,0:T(8,128)(2,1)S(1)}, u32[]{:S(2)}, u32[]{:S(2)}) collective-permute-start(bf16[1,64,768]{2,1,0:T(8,128)(2,1)} %get-tuple-element.34), channel_id=1, source_target_pairs={{0,5},{1,6},{2,7},{3,0},{4,1},{5,2},{6,3},{7,4},{8,13},{9,14},{10,... | collective-permute-start | bytes 294920 | tf_op jit(solution)/shard_map/ppermute | solution.py:22
  70.9 4.1 %collective-permute-done.2 = bf16[1,64,768]{2,1,0:T(8,128)(2,1)S(1)} collective-permute-done((bf16[1,64,768]{2,1,0:T(8,128)(2,1)}, bf16[1,64,768]{2,1,0:T(8,128)(2,1)S(1)}, u32[]{:S(2)}, u32[]{:S(2)}) %collective-permute-start.2) | collective-permute-done | bytes 98336 | tf_op jit(solution)/shard_map/ppermute | solution.py:22
  75.3 1.5 fusion.6
  76.8 1.2 copy.99
  78.1 5.4 %reduce.1 = bf16[512,768]{1,0:T(8,128)(2,1)S(1)} reduce(bf16[512,1,768]{2,1,0:T(2,128)(2,1)S(1)} %bitcast.39, bf16[]{:T(256)} %broadcast.14), dimensions={1}, to_apply=%bitcast.36.reduce_sub_computation | reduce | bytes 1572866
  83.5 0.2 reshape.41
  83.7 24.1 %all_to_all.33 = bf16[8,2,24576]{2,1,0:T(2,128)(2,1)S(1)} all-to-all(bf16[8,2,24576]{2,1,0:T(2,128)(2,1)S(1)} %reshape.41), channel_id=1, replica_groups=mesh['dp'=4,'seq'=8] {'seq'}, dimensions={0} | all-to-all | bytes 1572864 | tf_op jit(solution)/shard_map/all_to_all | solution.py:26
  107.8 0.8 reshape.42
  108.6 0.1 copy.84
  108.7 0.6 fusion.7
  109.3 1.0 copy.77
  110.3 3.6 %all-to-all-start.2 = ((bf16[8,64,768]{2,1,0:T(8,128)(2,1)}), bf16[8,64,768]{2,1,0:T(8,128)(2,1)S(1)}, u32[]{:S(2)}, u32[]{:S(2)}) async-start(bf16[8,64,768]{2,1,0:T(8,128)(2,1)} %copy.77), calls=%async_computation.2 | async-start | bytes 1572864 | tf_op jit(solution)/shard_map/all_to_all | solution.py:31
  113.9 0.0 all-reduce.2.cloned.1.call-start
  114.0 0.9 convolution_convert_fusion.3
  114.9 11.9 %psum.15 = bf16[64,8,8]{2,1,0:T(8,128)(2,1)S(1)} all-reduce(bf16[64,8,8]{2,1,0:T(8,128)(2,1)S(1)} %convolution_convert_fusion.3), channel_id=1, replica_groups=mesh['dp'=4,'seq'=8] {'dp'}, use_global_device_ids=true, to_apply=%region_1.2 | all-reduce | flops 4096 | bytes 16384 | tf_op jit(solution)/shard_map/psum | solution.py:36
  126.8 0.0 copy-start.4
  126.8 0.0 copy-start.6
  126.8 0.7 copy.81
  127.6 6.1 %all-to-all-done.2 = bf16[8,64,768]{2,1,0:T(8,128)(2,1)S(1)} async-done(((bf16[8,64,768]{2,1,0:T(8,128)(2,1)}), bf16[8,64,768]{2,1,0:T(8,128)(2,1)S(1)}, u32[]{:S(2)}, u32[]{:S(2)}) %all-to-all-start.2) | async-done | bytes 786464 | tf_op jit(solution)/shard_map/all_to_all | solution.py:31
  133.7 2.5 %fusion.9 = bf16[1,512,512]{2,1,0:T(8,128)(2,1)} fusion(bf16[512,768]{1,0:T(8,128)(2,1)S(1)} %bitcast.47, bf16[1,512,768]{2,1,0:T(8,128)(2,1)} %param.4), kind=kOutput, calls=%fused_computation.20 | convolution fusion | flops 402915328 | bytes 2097152 | tf_op jit(solution)/shard_map/bsc,brc->bsr/dot_general | solution.py:33
  136.2 0.0 all-reduce.2.cloned.1.call-update
  136.2 3.0 %fusion.5 = bf16[1,512,768]{2,1,0:T(8,128)(2,1)} fusion(bf16[1,512,768]{2,1,0:T(8,128)(2,1)S(1)} %copy-done.4, bf16[512,768]{1,0:T(8,128)(2,1)S(1)} %bitcast.48, bf16[1,1024,768]{2,1,0:T(8,128)(2,1)} %copy-done.7, s32[]{:T(128)S(6)} %select_n.26, bf16[1,512,512]{2,1,0:T(8,128)(2,1)S(1)} %copy-done, bf16[1,512,768]{2,1,0:T(8,128)(2,1)S(1)} %copy-done.6), kind=kOutput, calls=%fused_computation.9 | convolution fusion | flops 407764992 | bytes 4456452 | tf_op jit(solution)/shard_map/bsr,bsc->brc/dot_general | solution.py:32
  139.3 29.2 %all-reduce.2.cloned.1.call-done = bf16[1,512,512]{2,1,0:T(8,128)(2,1)} async-done(((bf16[1,512,512]{2,1,0:T(8,128)(2,1)}), bf16[1,512,512]{2,1,0:T(8,128)(2,1)}) %all-reduce.2.cloned.1.call-update) | async-done | bytes 524304 | tf_op jit(solution)/shard_map/psum | solution.py:35
  168.4 1.9 %copy.117 = bf16[1,512,512]{2,1,0:T(8,128)(2,1)} copy(bf16[1,512,512]{2,1,0:T(8,128)(2,1)} %all-reduce.2.cloned.1.call-done) | data formatting | bytes 1048576
  (34 shorter events, 0.2 us)
Async XLA Ops:
  7.2 1.0 copy-start
  17.1 8.4 %copy-start.8 = (bf16[64,8,8]{0,2,1:T(8,128)(2,1)S(1)}, bf16[64,8,8]{0,2,1:T(8,128)(2,1)}, u32[]{:S(2)}) copy-start(bf16[64,8,8]{0,2,1:T(8,128)(2,1)} %param.6) | copy-start | bytes 24580
  18.2 27.5 %all-to-all-start = ((bf16[8,2,24576]{2,1,0:T(2,128)(2,1)}), bf16[8,2,24576]{2,1,0:T(2,128)(2,1)S(1)}, u32[]{:S(2)}, u32[]{:S(2)}) async-start(bf16[8,2,24576]{2,1,0:T(2,128)(2,1)} %reshape.39), calls=%async_computation | async-start | bytes 1572864 | tf_op jit(solution)/shard_map/all_to_all | solution.py:12
  46.6 0.9 copy-start.1
  49.2 8.1 %collective-permute-start = (bf16[1,64,768]{2,1,0:T(8,128)(2,1)S(1)}, bf16[1,64,768]{2,1,0:T(8,128)(2,1)S(1)}, u32[]{:S(2)}, u32[]{:S(2)}) collective-permute-start(bf16[1,64,768]{2,1,0:T(8,128)(2,1)S(1)} %get-tuple-element.36), channel_id=1, source_target_pairs={{0,7},{1,0},{2,1},{3,2},{4,3},{5,4},{6,5},{7,6},{8,15},{9,8},{10,9... | collective-permute-start | bytes 294920 | tf_op jit(solution)/shard_map/ppermute | solution.py:22
  51.5 23.6 %collective-permute-start.6 = (bf16[1,64,768]{2,1,0:T(8,128)(2,1)S(1)}, bf16[1,64,768]{2,1,0:T(8,128)(2,1)S(1)}, u32[]{:S(2)}, u32[]{:S(2)}) collective-permute-start(bf16[1,64,768]{2,1,0:T(8,128)(2,1)S(1)} %get-tuple-element.30), channel_id=1, source_target_pairs={{0,1},{1,2},{2,3},{3,4},{4,5},{5,6},{6,7},{7,0},{8,9},{9,10},{10,1... | collective-permute-start | bytes 294920 | tf_op jit(solution)/shard_map/ppermute | solution.py:22
  51.5 23.6 %collective-permute-start.5 = (bf16[1,64,768]{2,1,0:T(8,128)(2,1)S(1)}, bf16[1,64,768]{2,1,0:T(8,128)(2,1)S(1)}, u32[]{:S(2)}, u32[]{:S(2)}) collective-permute-start(bf16[1,64,768]{2,1,0:T(8,128)(2,1)S(1)} %get-tuple-element.31), channel_id=1, source_target_pairs={{0,2},{1,3},{2,4},{3,5},{4,6},{5,7},{6,0},{7,1},{8,10},{9,11},{10,... | collective-permute-start | bytes 294920 | tf_op jit(solution)/shard_map/ppermute | solution.py:22
  52.1 23.0 %collective-permute-start.4 = (bf16[1,64,768]{2,1,0:T(8,128)(2,1)S(1)}, bf16[1,64,768]{2,1,0:T(8,128)(2,1)S(1)}, u32[]{:S(2)}, u32[]{:S(2)}) collective-permute-start(bf16[1,64,768]{2,1,0:T(8,128)(2,1)S(1)} %get-tuple-element.32), channel_id=1, source_target_pairs={{0,3},{1,4},{2,5},{3,6},{4,7},{5,0},{6,1},{7,2},{8,11},{9,12},{10,... | collective-permute-start | bytes 294920 | tf_op jit(solution)/shard_map/ppermute | solution.py:22
  53.2 21.9 %collective-permute-start.3 = (bf16[1,64,768]{2,1,0:T(8,128)(2,1)S(1)}, bf16[1,64,768]{2,1,0:T(8,128)(2,1)S(1)}, u32[]{:S(2)}, u32[]{:S(2)}) collective-permute-start(bf16[1,64,768]{2,1,0:T(8,128)(2,1)S(1)} %get-tuple-element.33), channel_id=1, source_target_pairs={{0,4},{1,5},{2,6},{3,7},{4,0},{5,1},{6,2},{7,3},{8,12},{9,13},{10,... | collective-permute-start | bytes 294920 | tf_op jit(solution)/shard_map/ppermute | solution.py:22
  57.3 17.9 %copy-start.3 = (bf16[1,512,768]{2,1,0:T(8,128)(2,1)S(1)}, bf16[1,512,768]{2,1,0:T(8,128)(2,1)}, u32[]{:S(2)}) copy-start(bf16[1,512,768]{2,1,0:T(8,128)(2,1)} %param.7) | copy-start | bytes 2359300
  57.3 17.9 %copy-start.5 = (bf16[1,512,768]{2,1,0:T(8,128)(2,1)S(1)}, bf16[1,512,768]{2,1,0:T(8,128)(2,1)}, u32[]{:S(2)}) copy-start(bf16[1,512,768]{2,1,0:T(8,128)(2,1)} %param.4) | copy-start | bytes 2359300
  57.3 5.7 %collective-permute-start.1 = (bf16[1,64,768]{2,1,0:T(8,128)(2,1)}, bf16[1,64,768]{2,1,0:T(8,128)(2,1)S(1)}, u32[]{:S(2)}, u32[]{:S(2)}) collective-permute-start(bf16[1,64,768]{2,1,0:T(8,128)(2,1)} %get-tuple-element.35), channel_id=1, source_target_pairs={{0,6},{1,7},{2,0},{3,1},{4,2},{5,3},{6,4},{7,5},{8,14},{9,15},{10,... | collective-permute-start | bytes 294920 | tf_op jit(solution)/shard_map/ppermute | solution.py:22
  63.0 12.0 %collective-permute-start.2 = (bf16[1,64,768]{2,1,0:T(8,128)(2,1)}, bf16[1,64,768]{2,1,0:T(8,128)(2,1)S(1)}, u32[]{:S(2)}, u32[]{:S(2)}) collective-permute-start(bf16[1,64,768]{2,1,0:T(8,128)(2,1)} %get-tuple-element.34), channel_id=1, source_target_pairs={{0,5},{1,6},{2,7},{3,0},{4,1},{5,2},{6,3},{7,4},{8,13},{9,14},{10,... | collective-permute-start | bytes 294920 | tf_op jit(solution)/shard_map/ppermute | solution.py:22
  75.3 1.5 copy-start.7
  109.3 4.7 %copy-start.2 = (bf16[1,512,768]{2,1,0:T(8,128)(2,1)S(1)}, bf16[1,512,768]{2,1,0:T(8,128)(2,1)}, u32[]{:S(2)}) copy-start(bf16[1,512,768]{2,1,0:T(8,128)(2,1)} %copy-done.1) | copy-start | bytes 2359300
  110.3 23.3 %all-to-all-start.2 = ((bf16[8,64,768]{2,1,0:T(8,128)(2,1)}), bf16[8,64,768]{2,1,0:T(8,128)(2,1)S(1)}, u32[]{:S(2)}, u32[]{:S(2)}) async-start(bf16[8,64,768]{2,1,0:T(8,128)(2,1)} %copy.77), calls=%async_computation.2 | async-start | bytes 1572864 | tf_op jit(solution)/shard_map/all_to_all | solution.py:31
  113.9 54.5 %all-reduce.2.cloned.1.call-start = ((), (), s32[]{:S(2)}) async-start(), calls=%async_computation.3 | async-start | bytes 1048576 | tf_op jit(solution)/shard_map/psum | solution.py:35
  126.8 9.4 %copy-start.4 = (bf16[1,512,768]{2,1,0:T(8,128)(2,1)S(1)}, bf16[1,512,768]{2,1,0:T(8,128)(2,1)}, u32[]{:S(2)}) copy-start(bf16[1,512,768]{2,1,0:T(8,128)(2,1)} %param.7) | copy-start | bytes 2359300
  126.8 9.4 %copy-start.6 = (bf16[1,512,768]{2,1,0:T(8,128)(2,1)S(1)}, bf16[1,512,768]{2,1,0:T(8,128)(2,1)}, u32[]{:S(2)}) copy-start(bf16[1,512,768]{2,1,0:T(8,128)(2,1)} %param.4) | copy-start | bytes 2359300
Sparse Core Ops, SparseCore 0:
  136.3 32.0 all-reduce.1
